TPU v7x, 32 devices: a whole 2x2x4 slice. The times are simulated.
32 devices in a mesh: row: 8 (over z, y), col: 4 (over x, core).
Axes of the slice: x: 2, y: 2, z: 4, core: 2. Of those that a mesh axis runs over, the one named last changes fastest.
Arguments:
- tokens: bfloat16 [512, 12288], P('col', 'row'), may hold values from -6 to 6
- in_weight: bfloat16 [12288, 24576], P('row', 'col'), may hold values from -0.0546875 to 0.0546875
- out_weight: bfloat16 [24576, 12288], P('col', 'row'), may hold values from -0.0390625 to 0.0390625
- out_grad: bfloat16 [512, 12288], P('col', 'row'), may hold values from -6 to 6
Outputs:
- layer_out: bfloat16 [512, 12288], P('col', 'row')
- token_grad: bfloat16 [512, 12288], P('col', 'row')
- first_grad: bfloat16 [12288, 24576], P('row', 'col')
- second_grad: bfloat16 [24576, 12288], P('col', 'row')
All inputs are finite; a program needn't handle non-finite values.
Results may differ from a plain program's by a relative error of at most 0.005.
Values may be sent and summed in bfloat16 or wider, within the bound.
A program may use at most 192 MiB of HBM per device.

v0:
```python
import jax
import jax.numpy as jnp
from jax import lax
from jax.sharding import PartitionSpec as P

gelu_c = 0.7978845608
gelu_k = 0.044715


def gelu_value(pre):
    inner = jnp.tanh(gelu_c * (pre + gelu_k * pre * pre * pre))
    return 0.5 * pre * (1.0 + inner)


def gelu_slope(pre):
    inner = jnp.tanh(gelu_c * (pre + gelu_k * pre * pre * pre))
    return 0.5 * (1.0 + inner) + 0.5 * pre * (1.0 - inner * inner) * gelu_c * (
        1.0 + 3.0 * gelu_k * pre * pre
    )


def dot_last(left, right):
    return lax.dot_general(
        left, right, (((1,), (1,)), ((), ())), preferred_element_type=jnp.float32
    )


def dot_first(left, right):
    return lax.dot_general(
        left, right, (((0,), (0,)), ((), ())), preferred_element_type=jnp.float32
    )


def per_device(tokens, in_weight, out_weight, out_grad):
    all_tokens = lax.all_gather(tokens, "col", axis=0, tiled=True)
    tok_total = all_tokens.shape[0]
    row_rows = tok_total // lax.axis_size("row")
    pre_total = lax.psum(jnp.dot(all_tokens, in_weight, preferred_element_type=jnp.float32), "row")
    all_hidden = gelu_value(pre_total).astype(jnp.bfloat16)
    pre_share = lax.dynamic_slice_in_dim(pre_total, lax.axis_index("row") * row_rows, row_rows, 0)
    block = all_hidden
    layer_out = lax.psum_scatter(
        jnp.dot(block, out_weight, preferred_element_type=jnp.float32),
        "col",
        scatter_dimension=0,
        tiled=True,
    ).astype(jnp.bfloat16)
    all_grads = lax.all_gather(out_grad, "col", axis=0, tiled=True)
    block = all_grads
    hid_share = lax.psum_scatter(
        dot_last(block, out_weight), "row", scatter_dimension=0, tiled=True
    )
    pre_grad = (hid_share * gelu_slope(pre_share)).astype(jnp.bfloat16)
    all_pre_grad = lax.all_gather(pre_grad, "row", axis=0, tiled=True)
    block = all_pre_grad
    token_grad = lax.psum_scatter(
        dot_last(block, in_weight), "col", scatter_dimension=0, tiled=True
    ).astype(jnp.bfloat16)
    first_grad = dot_first(all_tokens, all_pre_grad).astype(jnp.bfloat16)
    second_grad = dot_first(all_hidden, all_grads).astype(jnp.bfloat16)
    return (layer_out, token_grad, first_grad, second_grad)


def solution(mesh):
    return jax.shard_map(
        per_device,
        mesh=mesh,
        in_specs=(P("col", "row"), P("row", "col"), P("col", "row"), P("col", "row")),
        out_specs=(P("col", "row"), P("col", "row"), P("row", "col"), P("col", "row")),
        check_vma=False,
    )
```

profile of v0, /device:TPU:0, one launch (start us, length us, event | category | flops | bytes accessed | tf_op | source)
XLA Modules:
  0.0 859.1 jit_solution(6585336108579336340)
XLA Ops:
  7.2 0.0 all-gather.4.cloned.1.call-start
  7.2 0.7 all-gather.4.cloned.1.call-update
  7.9 0.0 all-gather.6.cloned.1.call-start
  7.9 0.7 all-gather.6.cloned.1.call-update
  8.6 0.0 all-reduce.2.cloned.1.call-start
  8.7 23.3 %all-gather.4.cloned.1.call-done = bf16[512,1536]{1,0:T(8,128)(2,1)} async-done(((bf16[128,1536]{1,0:T(8,128)(2,1)}), bf16[512,1536]{1,0:T(8,128)(2,1)}) %all-gather.4.cloned.1.call-update) | async-done | bytes 1572880 | tf_op jit(solution)/shard_map/all_gather | solution.py:35
  31.9 16.9 %fusion.16 = f32[512,6144]{1,0:T(8,128)} fusion(bf16[512,1536]{1,0:T(8,128)(2,1)} %all-gather.4.cloned.1.call-done, bf16[1536,6144]{1,0:T(8,128)(2,1)} %param.5), kind=kOutput, calls=%fused_computation.19 | convolution fusion | flops 9663676416 | bytes 33030144 | tf_op jit(solution)/shard_map/dot_general | solution.py:38
  48.8 0.0 all-reduce.2.cloned.1.call-update
  48.9 0.0 reduce-scatter.6.cloned.1.call-start
  48.9 4.3 all-gather.6.cloned.1.call-done
  53.2 16.9 %fusion.17 = f32[512,6144]{1,0:T(8,128)} fusion(bf16[512,1536]{1,0:T(8,128)(2,1)} %all-gather.6.cloned.1.call-done, bf16[6144,1536]{1,0:T(8,128)(2,1)} %param.6), kind=kOutput, calls=%fused_computation.20 | convolution fusion | flops 9663676416 | bytes 33030144 | tf_op jit(solution)/shard_map/dot_general | solution.py:23
  70.1 0.0 reduce-scatter.6.cloned.1.call-update
  70.2 0.0 all-gather.8.cloned.1.call-start
  70.2 385.3 %all-reduce.2.cloned.1.call-done = f32[512,6144]{1,0:T(8,128)} async-done(((f32[512,6144]{1,0:T(8,128)}), f32[512,6144]{1,0:T(8,128)}) %all-reduce.2.cloned.1.call-update) | async-done | bytes 12582928 | tf_op jit(solution)/shard_map/psum | solution.py:38
  455.5 210.9 %reduce-scatter.6.cloned.1.call-done = f32[64,6144]{1,0:T(8,128)} async-done(((f32[512,6144]{1,0:T(8,128)}), f32[64,6144]{1,0:T(8,128)}) %reduce-scatter.6.cloned.1.call-update) | async-done | bytes 1572880 | tf_op jit(solution)/shard_map/reduce_scatter | solution.py:50
  666.5 3.8 fusion.12
  670.2 0.0 all-gather.8.cloned.1.call-update
  670.2 0.2 reduce-scatter.4.cloned.1.call-start
  670.5 20.7 %fusion.14 = f32[512,1536]{1,0:T(8,128)} fusion(bf16[6144,1536]{1,0:T(8,128)(2,1)} %param.6, f32[512,6144]{1,0:T(8,128)} %all-reduce.2.cloned.1.call-done), kind=kOutput, calls=%fused_computation.18 | convolution fusion | flops 9691987968 | bytes 34603008 | tf_op jit(solution)/shard_map/dot_general | solution.py:43
  691.1 0.0 reduce-scatter.4.cloned.1.call-update
  691.1 0.0 copy-start.1
  691.1 0.0 reduce-scatter.8.cloned.1.call-start
  691.2 77.3 %all-gather.8.cloned.1.call-done = bf16[512,6144]{1,0:T(8,128)(2,1)} async-done(((bf16[64,6144]{1,0:T(8,128)(2,1)}), bf16[512,6144]{1,0:T(8,128)(2,1)}) %all-gather.8.cloned.1.call-update) | async-done | bytes 6291472 | tf_op jit(solution)/shard_map/all_gather | solution.py:54
  768.5 16.9 %fusion.18 = f32[512,1536]{1,0:T(8,128)} fusion(bf16[512,6144]{1,0:T(8,128)(2,1)} %all-gather.8.cloned.1.call-done, bf16[1536,6144]{1,0:T(8,128)(2,1)} %param.5), kind=kOutput, calls=%fused_computation.21 | convolution fusion | flops 9663676416 | bytes 28311552 | tf_op jit(solution)/shard_map/dot_general | solution.py:23
  785.4 0.0 reduce-scatter.8.cloned.1.call-update
  785.4 0.0 copy-done.1
  785.4 19.3 %convolution_convert_fusion = bf16[6144,1536]{1,0:T(8,128)(2,1)} fusion(bf16[512,1536]{1,0:T(8,128)(2,1)S(1)} %copy-done.1, f32[512,6144]{1,0:T(8,128)} %all-reduce.2.cloned.1.call-done), kind=kOutput, calls=%fused_computation | convolution fusion | flops 9701425152 | bytes 33030144 | tf_op jit(solution)/shard_map/dot_general | solution.py:29
  804.8 3.0 reduce-scatter.4.cloned.1.call-done
  807.8 1.9 convert_element_type.22
  809.7 16.0 %fusion = bf16[1536,6144]{0,1:T(8,128)(2,1)} fusion(bf16[512,6144]{1,0:T(8,128)(2,1)} %all-gather.8.cloned.1.call-done, bf16[512,1536]{1,0:T(8,128)(2,1)S(1)} %copy-done), kind=kOutput, calls=%fused_computation.2 | convolution fusion | flops 9673113600 | bytes 26738688 | tf_op jit(solution)/shard_map/dot_general | solution.py:29
  825.7 24.6 %copy.8 = bf16[1536,6144]{1,0:T(8,128)(2,1)} copy(bf16[1536,6144]{0,1:T(8,128)(2,1)} %fusion) | data formatting | bytes 37748736
  850.4 1.9 convert_element_type.24
  (3 shorter events, 0.0 us)
Async XLA Ops:
  7.2 24.8 %all-gather.4.cloned.1.call-start = ((), (), s32[]{:S(2)}) async-start(), calls=%async_computation.3 | async-start | bytes 1966080 | tf_op jit(solution)/shard_map/all_gather | solution.py:35
  7.9 45.3 %all-gather.6.cloned.1.call-start = ((), (), s32[]{:S(2)}) async-start(), calls=%async_computation.6 | async-start | bytes 1966080 | tf_op jit(solution)/shard_map/all_gather | solution.py:48
  8.6 446.9 %all-reduce.2.cloned.1.call-start = ((), (), s32[]{:S(2)}) async-start(), calls=%async_computation.4 | async-start | bytes 25165824 | tf_op jit(solution)/shard_map/psum | solution.py:38
  48.9 617.6 %reduce-scatter.6.cloned.1.call-start = ((), (), s32[]{:S(2)}) async-start(), calls=%async_computation.7 | async-start | bytes 14155776 | tf_op jit(solution)/shard_map/reduce_scatter | solution.py:50
  70.2 698.3 %all-gather.8.cloned.1.call-start = ((), (), s32[]{:S(2)}) async-start(), calls=%async_computation.8 | async-start | bytes 7077888 | tf_op jit(solution)/shard_map/all_gather | solution.py:54
  670.2 137.6 %reduce-scatter.4.cloned.1.call-start = ((), (), s32[]{:S(2)}) async-start(), calls=%async_computation.5 | async-start | bytes 3932160 | tf_op jit(solution)/shard_map/reduce_scatter | solution.py:42
  691.1 94.3 %copy-start.1 = (bf16[512,1536]{1,0:T(8,128)(2,1)S(1)}, bf16[512,1536]{1,0:T(8,128)(2,1)}, u32[]{:S(2)}) copy-start(bf16[512,1536]{1,0:T(8,128)(2,1)} %all-gather.6.cloned.1.call-done) | copy-start | bytes 4718596
  691.1 159.2 %reduce-scatter.8.cloned.1.call-start = ((), (), s32[]{:S(2)}) async-start(), calls=%async_computation.9 | async-start | bytes 3932160 | tf_op jit(solution)/shard_map/reduce_scatter | solution.py:56
  785.4 24.3 %copy-start = (bf16[512,1536]{1,0:T(8,128)(2,1)S(1)}, bf16[512,1536]{1,0:T(8,128)(2,1)}, u32[]{:S(2)}) copy-start(bf16[512,1536]{1,0:T(8,128)(2,1)} %all-gather.4.cloned.1.call-done) | copy-start | bytes 4718596
Sparse Core Ops, SparseCore 0:
  9.6 22.3 all-gather.3
  33.5 19.6 all-gather.5
  57.9 397.6 all-reduce.1
  460.0 206.4 reduce-scatter.5
  670.3 98.1 all-gather.7
  771.6 36.1 reduce-scatter.3
  810.3 37.9 reduce-scatter.7
where the time goes:
time: 860 us; the launch traced here: 859 us
  waiting for transfers between devices  706 us (82%)
  matrix products  107 us (12%)
  local copies, waits for them, and re-layouts  24.6 us (3%)
  between operations  14.2 us (2%)
    psum x1, waiting for transfers between devices, per_device(): lax.psum(jnp.dot(all_tokens, in_weight, preferred_element_type=jnp.float3...  385 us
    reduce_scatter x1, waiting for transfers between devices, per_device(): lax.psum_scatter(dot_last(block, out_weight), 'row', scatter_dimension=0,...  211 us
    all_gather x1, waiting for transfers between devices, per_device(): all_pre_grad = lax.all_gather(pre_grad, 'row', axis=0, tiled=True)  77.3 us
    dot_general x2, matrix products, dot_first(): lax.dot_general(left, right, (((0,), (0,)), ((), ())), preferred_element_...  35.3 us
    dot_general x2, matrix products, dot_last(): lax.dot_general(left, right, (((1,), (1,)), ((), ())), preferred_element_...  33.8 us
    unnamed x5, local copies, waits for them, and re-layouts  24.6 us
    all_gather x1, waiting for transfers between devices, per_device(): all_tokens = lax.all_gather(tokens, 'col', axis=0, tiled=True)  23.3 us
    dot_general x1, matrix products, per_device(): jnp.dot(block, out_weight, preferred_element_type=jnp.float32)  20.7 us
  transfers between devices with their start and end apart: 7, of which 6 were waited for; matrix products, arithmetic and copies ran while one was open for 16% of the time, Pallas kernels for 0%

commit v1 on v0

v1 whole, which is shorter than its diff:
```python
import functools

import jax
import jax.numpy as jnp
from jax import lax
from jax.experimental import pallas as pl
from jax.experimental.pallas import tpu as pltpu
from jax.sharding import PartitionSpec as P

gelu_c = 0.7978845608
gelu_k = 0.044715
f32, bf16 = jnp.float32, jnp.bfloat16
LAG = 2


def dot_last(left, right):
    return lax.dot_general(left, right, (((1,), (1,)), ((), ())), preferred_element_type=f32)


def dot_first(left, right):
    return lax.dot_general(left, right, (((0,), (0,)), ((), ())), preferred_element_type=f32)


def kernel(
    nz, ncol, chunks, width,
    tok, grad, w1, w2,
    out, lo, tg, tall, gall,
    part, yr, zr, w1a, w2a, w1b, w2b,
    wsem_a, wsem_b, gs, gr, ys, yrs, zs, zrs, azs, azr, ays, ayr,
):
    row, col = lax.axis_index("row"), lax.axis_index("col")
    z, y = row // 2, row % 2
    share, total = tok.shape[0], tall.shape[0]
    half = total // 2
    blk = half // nz
    rows_step = min(256, total)

    y_peer = {"row": z * 2 + (1 - y)}
    z_at = [lax.rem(z + d, nz) for d in range(1, nz)]
    z_peers = [{"row": p * 2 + y} for p in z_at]
    c_peers = [{"col": lax.rem(col + d, ncol)} for d in range(1, ncol)]

    def cols(c):
        return pl.ds(pl.multiple_of(c * width, width), width)

    def fetch(c, b1, b2, sem):
        slot = lax.rem(c, 2)
        return (
            pltpu.make_async_copy(w1.at[:, cols(c)], b1.at[slot], sem.at[slot, 0]),
            pltpu.make_async_copy(w2.at[cols(c), :], b2.at[slot], sem.at[slot, 1]),
        )

    for copy in fetch(0, w1a, w2a, wsem_a) + fetch(0, w1b, w2b, wsem_b):
        copy.start()

    barrier = pltpu.get_barrier_semaphore()
    peers = [y_peer] + z_peers + c_peers
    for peer in peers:
        pl.semaphore_signal(barrier, inc=1, device_id=peer, device_id_type=pl.DeviceIdType.MESH)
    pl.semaphore_wait(barrier, len(peers))

    def send(src, dst, s_sem, r_sem, peer):
        pltpu.make_async_remote_copy(
            src_ref=src, dst_ref=dst, send_sem=s_sem, recv_sem=r_sem,
            device_id=peer, device_id_type=pl.DeviceIdType.MESH,
        ).start()

    def drain(like, sem):
        pltpu.make_async_copy(like, like, sem).wait()

    mine = pl.ds(pl.multiple_of(col * share, share), share)
    for peer in c_peers:
        send(tok, tall.at[mine], gs.at[0], gr.at[0], peer)
        send(grad, gall.at[mine], gs.at[1], gr.at[1], peer)
    tall[mine] = tok[...]
    gall[mine] = grad[...]
    lo[...] = jnp.zeros_like(lo)
    tg[...] = jnp.zeros_like(tg)
    rest = pl.ds(0, (ncol - 1) * share)
    drain(tall.at[rest], gr.at[0])
    drain(gall.at[rest], gr.at[1])
    drain(tall.at[rest], gs.at[0])
    drain(gall.at[rest], gs.at[1])

    own_half = pl.ds(pl.multiple_of(y * half, half), half)
    other_half = pl.ds(pl.multiple_of((1 - y) * half, half), half)

    def block(p):
        return pl.ds(pl.multiple_of(y * half + p * blk, blk), blk)

    def front(c):
        slot = lax.rem(c, 2)

        @pl.when(c + 1 < chunks)
        def _():
            for copy in fetch(c + 1, w1a, w2a, wsem_a):
                copy.start()

        for copy in fetch(c, w1a, w2a, wsem_a):
            copy.wait()

        @pl.loop(0, total // rows_step)
        def _(i):
            r = pl.ds(pl.multiple_of(i * rows_step, rows_step), rows_step)
            part[0, r, cols(c)] = jnp.dot(
                tall[r, :], w1a[slot], preferred_element_type=f32
            ).astype(bf16)
            part[1, r, cols(c)] = dot_last(gall[r, :], w2a[slot]).astype(bf16)

        send(part.at[:, other_half, cols(c)], yr.at[:, :, cols(c)], ys.at[c], yrs.at[c], y_peer)

    def sum_y(c):
        drain(yr.at[:, :, cols(c)], yrs.at[c])
        drain(yr.at[:, :, cols(c)], ys.at[c])
        part[:, own_half, cols(c)] = (
            part[:, own_half, cols(c)].astype(f32) + yr[:, :, cols(c)].astype(f32)
        ).astype(bf16)
        for d, peer in enumerate(z_peers):
            send(
                part.at[:, block(z_at[d]), cols(c)], zr.at[d, :, :, cols(c)],
                zs.at[c], zrs.at[c], peer,
            )

    def sum_z(c):
        drain(zr.at[:, :, :, cols(c)], zrs.at[c])
        drain(zr.at[:, :, :, cols(c)], zs.at[c])
        both = part[:, block(z), cols(c)].astype(f32)
        for d in range(nz - 1):
            both = both + zr[d, :, :, cols(c)].astype(f32)
        pre, hid = both[0], both[1]
        t = jnp.tanh(gelu_c * (pre + gelu_k * pre * pre * pre))
        slope = 0.5 * (1.0 + t) + 0.5 * pre * (1.0 - t * t) * gelu_c * (
            1.0 + 3.0 * gelu_k * pre * pre
        )
        out[0, block(z), cols(c)] = (0.5 * pre * (1.0 + t)).astype(bf16)
        out[1, block(z), cols(c)] = (hid * slope).astype(bf16)
        at = out.at[:, block(z), cols(c)]
        for peer in z_peers:
            send(at, at, azs.at[c], azr.at[c], peer)

    def give_y(c):
        drain(zr.at[:, :, :, cols(c)], azr.at[c])
        drain(zr.at[:, :, :, cols(c)], azs.at[c])
        at = out.at[:, own_half, cols(c)]
        send(at, at, ays.at[c], ayr.at[c], y_peer)

    def back(c):
        slot = lax.rem(c, 2)

        @pl.when(c + 1 < chunks)
        def _():
            for copy in fetch(c + 1, w1b, w2b, wsem_b):
                copy.start()

        for copy in fetch(c, w1b, w2b, wsem_b):
            copy.wait()
        drain(yr.at[:, :, cols(c)], ayr.at[c])
        drain(yr.at[:, :, cols(c)], ays.at[c])

        @pl.loop(0, total // rows_step)
        def _(i):
            r = pl.ds(pl.multiple_of(i * rows_step, rows_step), rows_step)
            lo[r, :] += jnp.dot(out[0, r, cols(c)], w2b[slot], preferred_element_type=f32)
            tg[r, :] += dot_last(out[1, r, cols(c)], w1b[slot])

    stages = (front, sum_y, sum_z, give_y, back)

    @pl.loop(0, chunks + LAG * (len(stages) - 1))
    def _(s):
        for n, stage in enumerate(stages):
            c = s - n * LAG

            @pl.when(jnp.logical_and(c >= 0, c < chunks))
            def _(stage=stage, c=c):
                stage(c)


def per_device(nrow, ncol, tokens, in_weight, out_weight, out_grad):
    nz = nrow // 2
    share, feats = tokens.shape
    total = share * ncol
    hid = in_weight.shape[1]
    width = 256
    chunks = hid // width
    half, blk = total // 2, total // nrow
    vmem = pl.BlockSpec(memory_space=pltpu.VMEM)
    hbm = pl.BlockSpec(memory_space=pl.ANY)
    dma = pltpu.SemaphoreType.DMA
    both, lo, tg, all_tokens, all_grads = pl.pallas_call(
        functools.partial(kernel, nz, ncol, chunks, width),
        out_shape=(
            jax.ShapeDtypeStruct((2, total, hid), bf16),
            jax.ShapeDtypeStruct((total, feats), f32),
            jax.ShapeDtypeStruct((total, feats), f32),
            jax.ShapeDtypeStruct((total, feats), bf16),
            jax.ShapeDtypeStruct((total, feats), bf16),
        ),
        in_specs=[vmem, vmem, hbm, hbm],
        out_specs=(vmem,) * 5,
        scratch_shapes=[
            pltpu.VMEM((2, total, hid), bf16),
            pltpu.VMEM((2, half, hid), bf16),
            pltpu.VMEM((nz - 1, 2, blk, hid), bf16),
            pltpu.VMEM((2, feats, width), bf16),
            pltpu.VMEM((2, width, feats), bf16),
            pltpu.VMEM((2, feats, width), bf16),
            pltpu.VMEM((2, width, feats), bf16),
            dma((2, 2)),
            dma((2, 2)),
            dma((2,)),
            dma((2,)),
        ]
        + [dma((chunks,))] * 8,
        compiler_params=pltpu.CompilerParams(
            collective_id=0, has_side_effects=True, vmem_limit_bytes=62 * 1024 * 1024
        ),
        cost_estimate=pl.CostEstimate(
            flops=8 * total * feats * hid,
            bytes_accessed=8 * feats * hid + 4 * total * hid,
            transcendentals=blk * hid,
        ),
    )(tokens, out_grad, in_weight, out_weight)
    layer_out = lax.psum_scatter(lo, "col", scatter_dimension=0, tiled=True).astype(bf16)
    token_grad = lax.psum_scatter(tg, "col", scatter_dimension=0, tiled=True).astype(bf16)
    second_grad = dot_first(both[0], all_grads).astype(bf16)
    first_grad = dot_first(all_tokens, both[1]).astype(bf16)
    return (layer_out, token_grad, first_grad, second_grad)


def solution(mesh):
    return jax.shard_map(
        functools.partial(per_device, mesh.shape["row"], mesh.shape["col"]),
        mesh=mesh,
        in_specs=(P("col", "row"), P("row", "col"), P("col", "row"), P("col", "row")),
        out_specs=(P("col", "row"), P("col", "row"), P("row", "col"), P("col", "row")),
        check_vma=False,
    )
```

time: 860 us -> 439 us (0.51)
  waiting for transfers between devices: 706 us -> 47 us
  Pallas kernels: 0 us -> 341 us
  matrix products: 107 us -> 32 us
  local copies, waits for them, and re-layouts: 24.6 us -> 0.63 us
    psum x1 -> x0, waiting for transfers between devices: 385 us -> none  [per_device(): lax.psum(jnp.dot(all_tokens, in_weight, preferred_element_type=jnp.float3...]
    pallas_call x0 -> x1, Pallas kernels: none -> 341 us  [per_device(): pl.pallas_call(functools.partial(kernel, nz, ncol, chunks, width), out_sh...]
    reduce_scatter x3 -> x2, waiting for transfers between devices: 214 us -> 46.3 us  [the longest x1 38.8 us: per_device(): lax.psum_scatter(tg, 'col', scatter_dimension=0, tiled=True).astype(bf16)]
    all_gather x3 -> x0, waiting for transfers between devices: 105 us -> none  [the longest x1 77.3 us: per_device(): all_pre_grad = lax.all_gather(pre_grad, 'row', axis=0, tiled=True)]
    dot_general x4 -> x0, matrix products: 71.4 us -> none  [the longest x2 33.8 us: dot_last(): lax.dot_general(left, right, (((1,), (1,)), ((), ())), preferred_element_...]
    unnamed x5 -> x4, local copies, waits for them, and re-layouts: 24.6 us -> 0.63 us
  transfers between devices with their start and end apart: 7 -> 2, of which waited for: 6 -> 2; matrix products, arithmetic and copies ran while one was open for 16% -> 8% of each run, Pallas kernels for 0% -> 0%
where the time goes in v1:
time: 439 us
  Pallas kernels  341 us (78%)
  waiting for transfers between devices  47 us (11%)
  matrix products  32 us (7%)
  between operations  14.1 us (3%)
    pallas_call x1, Pallas kernels, per_device(): pl.pallas_call(functools.partial(kernel, nz, ncol, chunks, width), out_sh...  341 us
    reduce_scatter x1, waiting for transfers between devices, per_device(): lax.psum_scatter(tg, 'col', scatter_dimension=0, tiled=True).astype(bf16)  38.8 us
    dot_general x2, matrix products, dot_first(): lax.dot_general(left, right, (((0,), (0,)), ((), ())), preferred_element_...  32 us
  transfers between devices with their start and end apart: 2, of which 2 were waited for; matrix products, arithmetic and copies ran while one was open for 8% of the time, Pallas kernels for 0%

profile of v1, /device:TPU:0, one launch (start us, length us, event | category | flops | bytes accessed | tf_op | source)
XLA Modules:
  0.0 438.6 jit_solution(15333905334606034458)
XLA Ops:
  7.2 0.0 reduce-scatter.3.cloned.1.call-start
  7.2 341.0 %shard_map.75 = (bf16[2,512,6144]{2,1,0:T(8,128)(2,1)}, f32[512,1536]{1,0:T(8,128)}, f32[512,1536]{1,0:T(8,128)}, bf16[512,1536]{1,0:T(8,128)(2,1)}, bf16[512,1536]{1,0:T(8,128)(2,1)}) custom-call(bf16[128,1536]{1,0:T(8,128)(2,1)} %tok.1, bf16[128,1536]{1,0:T(8,128)(2,1)} %grad.1, bf16[1536,6144]{1,0:T(8,128)(2,1)} %w1.1, bf16[6144,1536]{1,0:T(8,128)(2,1)} %w2.1), custom_call_target="tpu_custom_call" | custom-call | flops 38654705664 | bytes 88080384 | tf_op jit(solution)/shard_map/pallas_call | solution.py:189
  348.2 0.0 copy-start
  348.2 0.0 reduce-scatter.3.cloned.1.call-update
  348.2 0.0 reduce-scatter.5.cloned.1.call-start
  348.3 0.7 reduce-scatter.5.cloned.1.call-update
  349.0 0.6 copy-done
  349.6 0.0 copy-start.1
  349.6 16.0 %convolution_convert_fusion = bf16[1536,6144]{1,0:T(8,128)(2,1)} fusion(bf16[512,1536]{1,0:T(8,128)(2,1)S(1)} %copy-done, bf16[2,512,6144]{2,1,0:T(8,128)(2,1)} %get-tuple-element.12), kind=kOutput, calls=%fused_computation | convolution fusion | flops 9673113600 | bytes 26738688 | tf_op jit(solution)/shard_map/dot_general | solution.py:21
  365.6 0.0 copy-done.1
  365.6 15.9 %convolution_convert_fusion.1 = bf16[6144,1536]{1,0:T(8,128)(2,1)} fusion(bf16[512,1536]{1,0:T(8,128)(2,1)S(1)} %copy-done.1, bf16[2,512,6144]{2,1,0:T(8,128)(2,1)} %get-tuple-element.12), kind=kOutput, calls=%fused_computation.1 | convolution fusion | flops 9673113600 | bytes 26738688 | tf_op jit(solution)/shard_map/dot_general | solution.py:21
  381.6 7.6 %reduce-scatter.3.cloned.1.call-done = f32[128,1536]{1,0:T(8,128)} async-done(((f32[512,1536]{1,0:T(8,128)}), f32[128,1536]{1,0:T(8,128)}) %reduce-scatter.3.cloned.1.call-update) | async-done | bytes 786448 | tf_op jit(solution)/shard_map/reduce_scatter | solution.py:223
  389.1 1.9 convert_element_type.12
  391.1 38.8 %reduce-scatter.5.cloned.1.call-done = f32[128,1536]{1,0:T(8,128)} async-done(((f32[512,1536]{1,0:T(8,128)}), f32[128,1536]{1,0:T(8,128)}) %reduce-scatter.5.cloned.1.call-update) | async-done | bytes 786448 | tf_op jit(solution)/shard_map/reduce_scatter | solution.py:224
  429.8 1.9 convert_element_type.13
Async XLA Ops:
  7.2 382.0 %reduce-scatter.3.cloned.1.call-start = ((), (), s32[]{:S(2)}) async-start(), calls=%async_computation.2 | async-start | bytes 3932160 | tf_op jit(solution)/shard_map/reduce_scatter | solution.py:223
  348.2 1.4 copy-start
  348.2 81.6 %reduce-scatter.5.cloned.1.call-start = ((), (), s32[]{:S(2)}) async-start(), calls=%async_computation.3 | async-start | bytes 3932160 | tf_op jit(solution)/shard_map/reduce_scatter | solution.py:224
  349.6 16.0 %copy-start.1 = (bf16[512,1536]{1,0:T(8,128)(2,1)S(1)}, bf16[512,1536]{1,0:T(8,128)(2,1)}, u32[]{:S(2)}) copy-start(bf16[512,1536]{1,0:T(8,128)(2,1)} %get-tuple-element.13) | copy-start | bytes 4718596
Sparse Core Ops, SparseCore 0:
  348.4 40.7 reduce-scatter.2
  391.8 37.9 reduce-scatter.4

commit v2 on v1

--- a/solution.py
+++ b/solution.py
@@ -24,8 +24,8 @@
 def kernel(
     nz, ncol, chunks, width,
     tok, grad, w1, w2,
-    out, lo, tg, tall, gall,
-    part, yr, zr, w1a, w2a, w1b, w2b,
+    out, ends, tall, gall,
+    part, mid, own, acc, yr, zr, w1a, w2a, w1b, w2b,
     wsem_a, wsem_b, gs, gr, ys, yrs, zs, zrs, azs, azr, ays, ayr,
 ):
     row, col = lax.axis_index("row"), lax.axis_index("col")
@@ -33,12 +33,18 @@
     share, total = tok.shape[0], tall.shape[0]
     half = total // 2
     blk = half // nz
-    rows_step = min(256, total)
+    rows_step = min(256, half)
+    feats = tok.shape[1]
+    keep = own.shape[0]
+    group, core = col // 2, col % 2
+    groups = ncol // 2
 
     y_peer = {"row": z * 2 + (1 - y)}
     z_at = [lax.rem(z + d, nz) for d in range(1, nz)]
     z_peers = [{"row": p * 2 + y} for p in z_at]
-    c_peers = [{"col": lax.rem(col + d, ncol)} for d in range(1, ncol)]
+    c_at = [lax.rem(group + d, groups) * 2 + core for d in range(1, groups)]
+    c_peers = [{"col": p} for p in c_at]
+    twin = {"col": group * 2 + (1 - core)}
 
     def cols(c):
         return pl.ds(pl.multiple_of(c * width, width), width)
@@ -54,7 +60,7 @@
         copy.start()
 
     barrier = pltpu.get_barrier_semaphore()
-    peers = [y_peer] + z_peers + c_peers
+    peers = [y_peer, twin] + z_peers + c_peers
     for peer in peers:
         pl.semaphore_signal(barrier, inc=1, device_id=peer, device_id_type=pl.DeviceIdType.MESH)
     pl.semaphore_wait(barrier, len(peers))
@@ -68,22 +74,31 @@
     def drain(like, sem):
         pltpu.make_async_copy(like, like, sem).wait()
 
-    mine = pl.ds(pl.multiple_of(col * share, share), share)
-    for peer in c_peers:
-        send(tok, tall.at[mine], gs.at[0], gr.at[0], peer)
-        send(grad, gall.at[mine], gs.at[1], gr.at[1], peer)
-    tall[mine] = tok[...]
-    gall[mine] = grad[...]
-    lo[...] = jnp.zeros_like(lo)
-    tg[...] = jnp.zeros_like(tg)
-    rest = pl.ds(0, (ncol - 1) * share)
-    drain(tall.at[rest], gr.at[0])
-    drain(gall.at[rest], gr.at[1])
-    drain(tall.at[rest], gs.at[0])
-    drain(gall.at[rest], gs.at[1])
+    def place(p):
+        return pl.ds(pl.multiple_of(p * share, share), share)
+
+    gathers = ((tok, tall), (grad, gall))
+    for n, (src, dst) in enumerate(gathers):
+        for peer in c_peers:
+            send(src, dst.at[place(col)], gs.at[n, 0], gr.at[n, 0], peer)
+    for n, (src, dst) in enumerate(gathers):
+        send(src, dst.at[place(col)], gs.at[n, 1], gr.at[n, 1], twin)
+    tall[place(col)] = tok[...]
+    gall[place(col)] = grad[...]
+    acc[...] = jnp.zeros_like(acc)
+    rest, one = pl.ds(0, (groups - 1) * share), pl.ds(0, share)
+    for n, (src, dst) in enumerate(gathers):
+        drain(dst.at[rest], gr.at[n, 0])
+        for p in c_at:
+            send(dst.at[place(p)], dst.at[place(p)], gs.at[n, 2], gr.at[n, 2], twin)
+    for n, (src, dst) in enumerate(gathers):
+        drain(dst.at[rest], gs.at[n, 0])
+        drain(dst.at[one], gs.at[n, 1])
+        drain(dst.at[one], gr.at[n, 1])
+        drain(dst.at[rest], gs.at[n, 2])
+        drain(dst.at[rest], gr.at[n, 2])
 
     own_half = pl.ds(pl.multiple_of(y * half, half), half)
-    other_half = pl.ds(pl.multiple_of((1 - y) * half, half), half)
 
     def block(p):
         return pl.ds(pl.multiple_of(y * half + p * blk, blk), blk)
@@ -99,32 +114,42 @@
         for copy in fetch(c, w1a, w2a, wsem_a):
             copy.wait()
 
-        @pl.loop(0, total // rows_step)
+        def rows(base, i):
+            return pl.ds(pl.multiple_of(base * half + i * rows_step, rows_step), rows_step)
+
+        @pl.loop(0, half // rows_step)
         def _(i):
-            r = pl.ds(pl.multiple_of(i * rows_step, rows_step), rows_step)
-            part[0, r, cols(c)] = jnp.dot(
+            r, to = rows(1 - y, i), rows(0, i)
+            part[0, to, cols(c)] = jnp.dot(
                 tall[r, :], w1a[slot], preferred_element_type=f32
             ).astype(bf16)
-            part[1, r, cols(c)] = dot_last(gall[r, :], w2a[slot]).astype(bf16)
-
-        send(part.at[:, other_half, cols(c)], yr.at[:, :, cols(c)], ys.at[c], yrs.at[c], y_peer)
+            part[1, to, cols(c)] = dot_last(gall[r, :], w2a[slot]).astype(bf16)
+
+        at = yr.at[:, :, cols(c)]
+        send(part.at[:, :, cols(c)], at, ys.at[c], yrs.at[c], y_peer)
+        mine = lax.rem(c, keep)
+
+        @pl.loop(0, half // rows_step)
+        def _(i):
+            r, to = rows(y, i), rows(0, i)
+            own[mine, 0, to, :] = jnp.dot(tall[r, :], w1a[slot], preferred_element_type=f32)
+            own[mine, 1, to, :] = dot_last(gall[r, :], w2a[slot])
 
     def sum_y(c):
         drain(yr.at[:, :, cols(c)], yrs.at[c])
         drain(yr.at[:, :, cols(c)], ys.at[c])
-        part[:, own_half, cols(c)] = (
-            part[:, own_half, cols(c)].astype(f32) + yr[:, :, cols(c)].astype(f32)
-        ).astype(bf16)
+        mine = lax.rem(c, keep)
+        total_y = own[mine] + yr[:, :, cols(c)].astype(f32)
+        own[mine] = total_y
+        mid[:, :, cols(c)] = total_y.astype(bf16)
         for d, peer in enumerate(z_peers):
-            send(
-                part.at[:, block(z_at[d]), cols(c)], zr.at[d, :, :, cols(c)],
-                zs.at[c], zrs.at[c], peer,
-            )
+            at = pl.ds(pl.multiple_of(z_at[d] * blk, blk), blk)
+            send(mid.at[:, at, cols(c)], zr.at[d, :, :, cols(c)], zs.at[c], zrs.at[c], peer)
 
     def sum_z(c):
         drain(zr.at[:, :, :, cols(c)], zrs.at[c])
         drain(zr.at[:, :, :, cols(c)], zs.at[c])
-        both = part[:, block(z), cols(c)].astype(f32)
+        both = own[lax.rem(c, keep), :, pl.ds(pl.multiple_of(z * blk, blk), blk), :]
         for d in range(nz - 1):
             both = both + zr[d, :, :, cols(c)].astype(f32)
         pre, hid = both[0], both[1]
@@ -160,8 +185,8 @@
         @pl.loop(0, total // rows_step)
         def _(i):
             r = pl.ds(pl.multiple_of(i * rows_step, rows_step), rows_step)
-            lo[r, :] += jnp.dot(out[0, r, cols(c)], w2b[slot], preferred_element_type=f32)
-            tg[r, :] += dot_last(out[1, r, cols(c)], w1b[slot])
+            acc[r, :feats] += jnp.dot(out[0, r, cols(c)], w2b[slot], preferred_element_type=f32)
+            acc[r, feats:] += dot_last(out[1, r, cols(c)], w1b[slot])
 
     stages = (front, sum_y, sum_z, give_y, back)
 
@@ -173,6 +198,8 @@
             @pl.when(jnp.logical_and(c >= 0, c < chunks))
             def _(stage=stage, c=c):
                 stage(c)
+
+    ends[...] = acc[...].astype(bf16)
 
 
 def per_device(nrow, ncol, tokens, in_weight, out_weight, out_grad):
@@ -186,19 +213,21 @@
     vmem = pl.BlockSpec(memory_space=pltpu.VMEM)
     hbm = pl.BlockSpec(memory_space=pl.ANY)
     dma = pltpu.SemaphoreType.DMA
-    both, lo, tg, all_tokens, all_grads = pl.pallas_call(
+    both, ends, all_tokens, all_grads = pl.pallas_call(
         functools.partial(kernel, nz, ncol, chunks, width),
         out_shape=(
             jax.ShapeDtypeStruct((2, total, hid), bf16),
-            jax.ShapeDtypeStruct((total, feats), f32),
-            jax.ShapeDtypeStruct((total, feats), f32),
+            jax.ShapeDtypeStruct((total, 2 * feats), bf16),
             jax.ShapeDtypeStruct((total, feats), bf16),
             jax.ShapeDtypeStruct((total, feats), bf16),
         ),
         in_specs=[vmem, vmem, hbm, hbm],
-        out_specs=(vmem,) * 5,
+        out_specs=(vmem,) * 4,
         scratch_shapes=[
-            pltpu.VMEM((2, total, hid), bf16),
+            pltpu.VMEM((2, half, hid), bf16),
+            pltpu.VMEM((2, half, hid), bf16),
+            pltpu.VMEM((2 * LAG + 1, 2, half, width), f32),
+            pltpu.VMEM((total, 2 * feats), f32),
             pltpu.VMEM((2, half, hid), bf16),
             pltpu.VMEM((nz - 1, 2, blk, hid), bf16),
             pltpu.VMEM((2, feats, width), bf16),
@@ -207,8 +236,8 @@
             pltpu.VMEM((2, width, feats), bf16),
             dma((2, 2)),
             dma((2, 2)),
-            dma((2,)),
-            dma((2,)),
+            dma((2, 3)),
+            dma((2, 3)),
         ]
         + [dma((chunks,))] * 8,
         compiler_params=pltpu.CompilerParams(
@@ -220,11 +249,10 @@
             transcendentals=blk * hid,
         ),
     )(tokens, out_grad, in_weight, out_weight)
-    layer_out = lax.psum_scatter(lo, "col", scatter_dimension=0, tiled=True).astype(bf16)
-    token_grad = lax.psum_scatter(tg, "col", scatter_dimension=0, tiled=True).astype(bf16)
+    ends = lax.psum_scatter(ends, "col", scatter_dimension=0, tiled=True)
     second_grad = dot_first(both[0], all_grads).astype(bf16)
     first_grad = dot_first(all_tokens, both[1]).astype(bf16)
-    return (layer_out, token_grad, first_grad, second_grad)
+    return (ends[:, :feats], ends[:, feats:], first_grad, second_grad)
 
 
 def solution(mesh):

time: 439 us -> 380 us (0.87)
  waiting for transfers between devices: 47 us -> 5.3 us
  Pallas kernels: 341 us -> 325 us
    reduce_scatter x2 -> x1, waiting for transfers between devices: 46.3 us -> 5.29 us  [per_device(): ends = lax.psum_scatter(ends, 'col', scatter_dimension=0, tiled=True)]
    pallas_call x1, Pallas kernels: 341 us -> 325 us  [per_device(): pl.pallas_call(functools.partial(kernel, nz, ncol, chunks, width), out_sh...]
  transfers between devices with their start and end apart: 2 -> 1, of which waited for: 2 -> 1; matrix products, arithmetic and copies ran while one was open for 8% -> 9% of each run, Pallas kernels for 0% -> 0%
where the time goes in v2:
time: 380 us
  Pallas kernels  325 us (86%)
  matrix products  32.9 us (9%)
  between operations  14 us (4%)
  waiting for transfers between devices  5.3 us (1%)
    pallas_call x1, Pallas kernels, per_device(): pl.pallas_call(functools.partial(kernel, nz, ncol, chunks, width), out_sh...  325 us
    dot_general x2, matrix products, dot_first(): lax.dot_general(left, right, (((0,), (0,)), ((), ())), preferred_element_...  32.9 us
  transfers between devices with their start and end apart: 1, of which 1 were waited for; matrix products, arithmetic and copies ran while one was open for 9% of the time, Pallas kernels for 0%

profile of v2, /device:TPU:0, one launch (start us, length us, event | category | flops | bytes accessed | tf_op | source)
XLA Modules:
  0.0 379.8 jit_solution(15778982665967725207)
XLA Ops:
  7.2 0.0 reduce-scatter.2.cloned.1.call-start
  7.2 325.4 %shard_map.75 = (bf16[2,512,6144]{2,1,0:T(8,128)(2,1)}, bf16[512,3072]{1,0:T(8,128)(2,1)}, bf16[512,1536]{1,0:T(8,128)(2,1)}, bf16[512,1536]{1,0:T(8,128)(2,1)}) custom-call(bf16[128,1536]{1,0:T(8,128)(2,1)} %tok.1, bf16[128,1536]{1,0:T(8,128)(2,1)} %grad.1, bf16[1536,6144]{1,0:T(8,128)(2,1)} %w1.1, bf16[6144,1536]{1,0:T(8,128)(2,1)} %w2.1), custom_call_target="tpu_custom_call" | custom-call | flops 38654705664 | bytes 88080384 | tf_op jit(solution)/shard_map/pallas_call | solution.py:216
  332.6 0.0 reduce-scatter.2.cloned.1.call-update
  332.7 0.0 copy-start
  332.7 16.5 %convolution_convert_fusion = bf16[1536,6144]{1,0:T(8,128)(2,1)} fusion(bf16[512,1536]{1,0:T(8,128)(2,1)} %get-tuple-element.9, bf16[2,512,6144]{2,1,0:T(8,128)(2,1)} %get-tuple-element.10), kind=kOutput, calls=%fused_computation | convolution fusion | flops 9673113600 | bytes 26738688 | tf_op jit(solution)/shard_map/dot_general | solution.py:21
  349.1 0.0 copy-done
  349.1 16.5 %convolution_convert_fusion.1 = bf16[6144,1536]{1,0:T(8,128)(2,1)} fusion(bf16[512,1536]{1,0:T(8,128)(2,1)S(1)} %copy-done, bf16[2,512,6144]{2,1,0:T(8,128)(2,1)} %get-tuple-element.10), kind=kOutput, calls=%fused_computation.1 | convolution fusion | flops 9673113600 | bytes 26738688 | tf_op jit(solution)/shard_map/dot_general | solution.py:21
  365.6 5.3 %reduce-scatter.2.cloned.1.call-done = bf16[128,3072]{1,0:T(8,128)(2,1)} async-done(((bf16[512,3072]{1,0:T(8,128)(2,1)}), bf16[128,3072]{1,0:T(8,128)(2,1)}) %reduce-scatter.2.cloned.1.call-update) | async-done | bytes 786448 | tf_op jit(solution)/shard_map/reduce_scatter | solution.py:252
  370.9 2.0 fusion.4
Async XLA Ops:
  7.2 363.7 %reduce-scatter.2.cloned.1.call-start = ((), (), s32[]{:S(2)}) async-start(), calls=%async_computation.1 | async-start | bytes 3932160 | tf_op jit(solution)/shard_map/reduce_scatter | solution.py:252
  332.7 16.5 %copy-start = (bf16[512,1536]{1,0:T(8,128)(2,1)S(1)}, bf16[512,1536]{1,0:T(8,128)(2,1)}, u32[]{:S(2)}) copy-start(bf16[512,1536]{1,0:T(8,128)(2,1)} %get-tuple-element.11) | copy-start | bytes 4718596
Sparse Core Ops, SparseCore 0:
  332.8 38.0 reduce-scatter.1

commit v3 on v2

--- a/solution.py
+++ b/solution.py
@@ -101,7 +101,88 @@
     own_half = pl.ds(pl.multiple_of(y * half, half), half)
 
     def block(p):
-        return pl.ds(pl.multiple_of(y * half + p * blk, blk), blk)
+        return pl.ds(pl.multiple_of(p * blk, blk), blk)
+
+    def is_wide(c):
+        return lax.rem(c, 3) == 1
+
+    z_right = {"row": lax.rem(z + 1, nz) * 2 + y}
+    z_left = {"row": lax.rem(z + nz - 1, nz) * 2 + y}
+
+    def hop_like(c, wide):
+        return yr.at[:, pl.ds(0, 2 * blk if wide else blk), cols(c)]
+
+    def hop_at(c, p, wide):
+        return out.at[:, :, block(p), cols(c)] if wide else out.at[:, y, block(p), cols(c)]
+
+    def hop_send(c, h, wide):
+        @pl.when(jnp.logical_and(z - h >= 0, z + 1 < nz))
+        def _():
+            at = hop_at(c, z - h, wide)
+            send(at, at, azs.at[c, 0, h], azr.at[c, 0, h], z_right)
+
+        @pl.when(jnp.logical_and(z + h < nz, z >= 1))
+        def _():
+            at = hop_at(c, z + h, wide)
+            send(at, at, azs.at[c, 1, h], azr.at[c, 1, h], z_left)
+
+    def hop_wait(c, h, wide):
+        like = hop_like(c, wide)
+
+        @pl.when(z - 1 - h >= 0)
+        def _():
+            drain(like, azr.at[c, 0, h])
+
+        @pl.when(z + 1 + h < nz)
+        def _():
+            drain(like, azr.at[c, 1, h])
+
+        @pl.when(jnp.logical_and(z - h >= 0, z + 1 < nz))
+        def _():
+            drain(like, azs.at[c, 0, h])
+
+        @pl.when(jnp.logical_and(z + h < nz, z >= 1))
+        def _():
+            drain(like, azs.at[c, 1, h])
+
+    def y_send(c, wide):
+        at = out.at[:, y, block(z), cols(c)] if wide else out.at[:, y, :, cols(c)]
+        send(at, at, ays.at[c], ayr.at[c], y_peer)
+
+    def y_wait(c, wide):
+        like = hop_like(c, False) if wide else yr.at[:, :, cols(c)]
+        drain(like, ayr.at[c])
+        drain(like, ays.at[c])
+
+    def per_mode(c, f):
+        for wide in (False, True):
+            @pl.when(is_wide(c) == wide)
+            def _(wide=wide):
+                f(wide)
+
+    def spread(j, c):
+        def f(wide):
+            if wide:
+                if j == 1:
+                    y_wait(c, wide)
+                elif j > 1:
+                    hop_wait(c, j - 2, wide)
+                if j == 0:
+                    y_send(c, wide)
+                else:
+                    hop_send(c, j - 1, wide)
+            else:
+                if j > 0:
+                    hop_wait(c, j - 1, wide)
+                if j < nz - 1:
+                    hop_send(c, j, wide)
+                else:
+                    y_send(c, wide)
+
+        per_mode(c, f)
+
+    def last_wait(c):
+        per_mode(c, lambda wide: hop_wait(c, nz - 2, wide) if wide else y_wait(c, wide))
 
     def front(c):
         slot = lax.rem(c, 2)
@@ -157,17 +238,9 @@
         slope = 0.5 * (1.0 + t) + 0.5 * pre * (1.0 - t * t) * gelu_c * (
             1.0 + 3.0 * gelu_k * pre * pre
         )
-        out[0, block(z), cols(c)] = (0.5 * pre * (1.0 + t)).astype(bf16)
-        out[1, block(z), cols(c)] = (hid * slope).astype(bf16)
-        at = out.at[:, block(z), cols(c)]
-        for peer in z_peers:
-            send(at, at, azs.at[c], azr.at[c], peer)
-
-    def give_y(c):
-        drain(zr.at[:, :, :, cols(c)], azr.at[c])
-        drain(zr.at[:, :, :, cols(c)], azs.at[c])
-        at = out.at[:, own_half, cols(c)]
-        send(at, at, ays.at[c], ayr.at[c], y_peer)
+        out[0, y, block(z), cols(c)] = (0.5 * pre * (1.0 + t)).astype(bf16)
+        out[1, y, block(z), cols(c)] = (hid * slope).astype(bf16)
+        spread(0, c)
 
     def back(c):
         slot = lax.rem(c, 2)
@@ -179,16 +252,18 @@
 
         for copy in fetch(c, w1b, w2b, wsem_b):
             copy.wait()
-        drain(yr.at[:, :, cols(c)], ayr.at[c])
-        drain(yr.at[:, :, cols(c)], ays.at[c])
+        last_wait(c)
 
         @pl.loop(0, total // rows_step)
         def _(i):
             r = pl.ds(pl.multiple_of(i * rows_step, rows_step), rows_step)
-            acc[r, :feats] += jnp.dot(out[0, r, cols(c)], w2b[slot], preferred_element_type=f32)
-            acc[r, feats:] += dot_last(out[1, r, cols(c)], w1b[slot])
-
-    stages = (front, sum_y, sum_z, give_y, back)
+            side = i // (half // rows_step)
+            at = pl.ds(pl.multiple_of(i * rows_step - side * half, rows_step), rows_step)
+            acc[r, :feats] += jnp.dot(out[0, side, at, cols(c)], w2b[slot], preferred_element_type=f32)
+            acc[r, feats:] += dot_last(out[1, side, at, cols(c)], w1b[slot])
+
+    spreads = tuple(functools.partial(spread, j) for j in range(1, nz))
+    stages = (front, sum_y, sum_z) + spreads + (back,)
 
     @pl.loop(0, chunks + LAG * (len(stages) - 1))
     def _(s):
@@ -216,7 +291,7 @@
     both, ends, all_tokens, all_grads = pl.pallas_call(
         functools.partial(kernel, nz, ncol, chunks, width),
         out_shape=(
-            jax.ShapeDtypeStruct((2, total, hid), bf16),
+            jax.ShapeDtypeStruct((2, 2, half, hid), bf16),
             jax.ShapeDtypeStruct((total, 2 * feats), bf16),
             jax.ShapeDtypeStruct((total, feats), bf16),
             jax.ShapeDtypeStruct((total, feats), bf16),
@@ -239,7 +314,9 @@
             dma((2, 3)),
             dma((2, 3)),
         ]
-        + [dma((chunks,))] * 8,
+        + [dma((chunks,))] * 4
+        + [dma((chunks, 2, nz - 1))] * 2
+        + [dma((chunks,))] * 2,
         compiler_params=pltpu.CompilerParams(
             collective_id=0, has_side_effects=True, vmem_limit_bytes=62 * 1024 * 1024
         ),
@@ -249,6 +326,7 @@
             transcendentals=blk * hid,
         ),
     )(tokens, out_grad, in_weight, out_weight)
+    both = both.reshape(2, total, hid)
     ends = lax.psum_scatter(ends, "col", scatter_dimension=0, tiled=True)
     second_grad = dot_first(both[0], all_grads).astype(bf16)
     first_grad = dot_first(all_tokens, both[1]).astype(bf16)

time: 380 us -> 348 us (0.916)
  Pallas kernels: 325 us -> 293 us
  local copies, waits for them, and re-layouts: 2.04 us -> 10.9 us
  waiting for transfers between devices: 5.3 us -> 0.02 us
    pallas_call x1, Pallas kernels: 325 us -> 293 us  [per_device(): pl.pallas_call(functools.partial(kernel, nz, ncol, chunks, width), out_sh...]
    slice x0 -> x1, local copies, waits for them, and re-layouts: none -> 8.89 us  [per_device(): second_grad = dot_first(both[0], all_grads).astype(bf16)]
    reduce_scatter x1, waiting for transfers between devices: 5.29 us -> 0.01 us  [per_device(): ends = lax.psum_scatter(ends, 'col', scatter_dimension=0, tiled=True)]
  transfers between devices with their start and end apart: 1 -> 1, of which waited for: 1 -> 0; matrix products, arithmetic and copies ran while one was open for 9% -> 11% of each run, Pallas kernels for 0% -> 0%
where the time goes in v3:
time: 348 us
  Pallas kernels  293 us (84%)
  matrix products  29.4 us (8%)
  between operations  14 us (4%)
  local copies, waits for them, and re-layouts  10.9 us (3%)
    pallas_call x1, Pallas kernels, per_device(): pl.pallas_call(functools.partial(kernel, nz, ncol, chunks, width), out_sh...  293 us
    dot_general x2, matrix products, dot_first(): lax.dot_general(left, right, (((0,), (0,)), ((), ())), preferred_element_...  29.4 us
    slice x1, local copies, waits for them, and re-layouts, per_device(): second_grad = dot_first(both[0], all_grads).astype(bf16)  8.89 us
  transfers between devices with their start and end apart: 1, of which 0 were waited for; matrix products, arithmetic and copies ran while one was open for 11% of the time, Pallas kernels for 0%

profile of v3, /device:TPU:0, one launch (start us, length us, event | category | flops | bytes accessed | tf_op | source)
XLA Modules:
  0.0 347.7 jit_solution(285341609090157634)
XLA Ops:
  7.2 0.0 reduce-scatter.2.cloned.1.call-start
  7.2 293.2 %shard_map.75 = (bf16[2,2,256,6144]{3,2,1,0:T(8,128)(2,1)}, bf16[512,3072]{1,0:T(8,128)(2,1)}, bf16[512,1536]{1,0:T(8,128)(2,1)}, bf16[512,1536]{1,0:T(8,128)(2,1)}) custom-call(bf16[128,1536]{1,0:T(8,128)(2,1)} %tok.1, bf16[128,1536]{1,0:T(8,128)(2,1)} %grad.1, bf16[1536,6144]{1,0:T(8,128)(2,1)} %w1.1, bf16[6144,1536]{1,0:T(8,128)(2,1)} %w2.1), custom_call_target="tpu_custom_call" | custom-call | flops 38654705664 | bytes 88080384 | tf_op jit(solution)/shard_map/pallas_call | solution.py:291
  300.5 0.0 reduce-scatter.2.cloned.1.call-update
  300.5 0.0 copy-start
  300.5 8.9 %fusion = (bf16[1,2,256,6144]{3,2,1,0:T(8,128)(2,1)S(1)}, bf16[1,2,256,6144]{3,2,1,0:T(8,128)(2,1)}) fusion(bf16[2,2,256,6144]{3,2,1,0:T(8,128)(2,1)} %get-tuple-element.10), kind=kLoop, calls=%fused_computation.2 | loop fusion | bytes 25165824 | tf_op jit(solution)/shard_map/slice | solution.py:331
  309.4 0.0 copy-done
  309.4 0.0 copy-start.1
  309.4 16.1 %convolution_convert_fusion = bf16[1536,6144]{1,0:T(8,128)(2,1)} fusion(bf16[512,1536]{1,0:T(8,128)(2,1)S(1)} %copy-done, bf16[512,6144]{1,0:T(8,128)(2,1)} %bitcast.7), kind=kOutput, calls=%fused_computation | convolution fusion | flops 9673113600 | bytes 26738688 | tf_op jit(solution)/shard_map/dot_general | solution.py:21
  325.5 0.0 copy-done.1
  325.5 13.2 %convolution_convert_fusion.1 = bf16[6144,1536]{1,0:T(8,128)(2,1)} fusion(bf16[512,6144]{1,0:T(8,128)(2,1)S(1)} %bitcast.6, bf16[512,1536]{1,0:T(8,128)(2,1)S(1)} %copy-done.1), kind=kOutput, calls=%fused_computation.1 | convolution fusion | flops 9673113600 | bytes 26738688 | tf_op jit(solution)/shard_map/dot_general | solution.py:21
  338.8 0.0 reduce-scatter.2.cloned.1.call-done
  338.8 2.0 fusion.1
Async XLA Ops:
  7.2 331.6 %reduce-scatter.2.cloned.1.call-start = ((), (), s32[]{:S(2)}) async-start(), calls=%async_computation.1 | async-start | bytes 3932160 | tf_op jit(solution)/shard_map/reduce_scatter | solution.py:330
  300.5 8.9 %copy-start = (bf16[512,1536]{1,0:T(8,128)(2,1)S(1)}, bf16[512,1536]{1,0:T(8,128)(2,1)}, u32[]{:S(2)}) copy-start(bf16[512,1536]{1,0:T(8,128)(2,1)} %get-tuple-element.9) | copy-start | bytes 4718596
  309.4 16.2 %copy-start.1 = (bf16[512,1536]{1,0:T(8,128)(2,1)S(1)}, bf16[512,1536]{1,0:T(8,128)(2,1)}, u32[]{:S(2)}) copy-start(bf16[512,1536]{1,0:T(8,128)(2,1)} %get-tuple-element.11) | copy-start | bytes 4718596
Sparse Core Ops, SparseCore 0:
  300.6 36.8 reduce-scatter.1
